TPU v7x, 32 devices: a whole 2x2x4 slice. The times are simulated.
32 devices in a mesh: cuts: 8 (over y, x, core), pencil: 4 (over z).
Axes of the slice: x: 2, y: 2, z: 4, core: 2. Of those that a mesh axis runs over, the one named last changes fastest.
Arguments:
- wavefunctions: bfloat16 [32, 9216, 192], P('cuts', 'pencil'), may hold values from -8 to 8
- potential: float32 [192, 192, 192], P('pencil'), may hold values from -6 to 6
- keep_mask: int32 [8, 2, 2], P('cuts'), may hold values 0 or 1
- stick_map: int32 [9216], P('pencil'), may hold values from 0 to 2303, as said below
Outputs:
- hamiltonian_bands: bfloat16 [32, 9216, 192], P('cuts', 'pencil')
Inputs may be any that keep to these rules, and one draw needn't show every extreme that they name: `stick_map`: each block of 2304 consecutive entries (one index of pencil) is a permutation of 0 to 2303.
All inputs are finite; a program needn't handle non-finite values. No bound on the sum of `keep_mask` on one device may be relied on, other than what follows from the above.
Results may differ from a plain program's by a relative error of at most 0.0065.
Values may be sent and summed in bfloat16 or wider, within the bound.
A program may use at most 256 MiB of HBM per device.

v0:
```python
import math

import jax
import jax.numpy as jnp
from jax import lax
from jax.sharding import PartitionSpec as P

GRID = 192
EDGE = 2
GBOX = 96


def from_behind(block, axis, distance):
    devices = range(lax.axis_size(axis))
    route = [(i - distance, i) for i in devices if i - distance in devices]
    return lax.ppermute(block, axis, route)


def dft_tables(box_size, length):
    frequency = jnp.arange(box_size, dtype=jnp.float32) - float(box_size // 2)
    points = jnp.arange(length, dtype=jnp.float32)
    phases = 2.0 * math.pi / length * jnp.mod(frequency[:, None] * points[None, :], float(length))
    ahead_scale = 1.0 / math.sqrt(box_size)
    behind_scale = math.sqrt(box_size) / length
    ahead_cos = (jnp.cos(phases) * ahead_scale).astype(jnp.bfloat16)
    ahead_sin = (jnp.sin(phases) * ahead_scale).astype(jnp.bfloat16)
    behind_cos = (jnp.cos(phases).T * behind_scale).astype(jnp.bfloat16)
    behind_sin = (-jnp.sin(phases).T * behind_scale).astype(jnp.bfloat16)
    return (ahead_cos, ahead_sin, behind_cos, behind_sin)


def last_matrix(cos_table, sin_table):
    upper_rows = jnp.concatenate([cos_table, sin_table], axis=1)
    lower_rows = jnp.concatenate([-sin_table, cos_table], axis=1)
    return jnp.concatenate([upper_rows, lower_rows], axis=0)


def combine_halves(cos_part, sin_part):
    middle = cos_part.shape[-1] // 2
    real_part = cos_part[..., :middle] - sin_part[..., middle:]
    imag_part = sin_part[..., :middle] + cos_part[..., middle:]
    return jnp.concatenate([real_part, imag_part], axis=-1)


def along_axis(values, cos_table, sin_table, pattern):
    cos_part = jnp.einsum(pattern, values, cos_table, preferred_element_type=jnp.float32)
    sin_part = jnp.einsum(pattern, values, sin_table, preferred_element_type=jnp.float32)
    return combine_halves(cos_part, sin_part)


def along_last(values, matrix):
    return jnp.einsum("bxyc,cd->bxyd", values, matrix, preferred_element_type=jnp.float32)


def kinetic_table(box_size, row_start, column_count):
    center = box_size // 2
    freq_rows = jnp.arange(box_size, dtype=jnp.float32) - center
    freq_cols = (row_start + jnp.arange(column_count, dtype=jnp.int32)).astype(jnp.float32) - center
    freq_depth = jnp.arange(box_size, dtype=jnp.float32) - center
    freq_depth = jnp.concatenate([freq_depth, freq_depth])
    squares = (
        freq_rows[:, None, None] ** 2
        + freq_cols[None, :, None] ** 2
        + freq_depth[None, None, :] ** 2
    )
    return 0.5 * squares / float(center * center)


def local(wavefunctions, potential, keep_mask, stick_map):
    bands_dev, sticks_dev, row_width = wavefunctions.shape
    middle = row_width // 2
    rows_local = sticks_dev // GBOX
    precise = lax.Precision.HIGHEST
    upper_edge = wavefunctions[bands_dev - EDGE :]
    lower_edge = wavefunctions[:EDGE].astype(jnp.float32)
    neighbor = from_behind(upper_edge, "cuts", 1).astype(jnp.float32)
    correlation_real = jnp.einsum("jgc,igc->ji", neighbor, lower_edge, precision=precise)
    correlation_imag = jnp.einsum(
        "jgc,igc->ji", neighbor[..., :middle], lower_edge[..., middle:], precision=precise
    ) - jnp.einsum(
        "jgc,igc->ji", neighbor[..., middle:], lower_edge[..., :middle], precision=precise
    )
    neighbor_norms = jnp.sum(neighbor * neighbor, axis=(1, 2))
    correlation_real, correlation_imag, neighbor_norms = lax.psum(
        (correlation_real, correlation_imag, neighbor_norms), "pencil"
    )
    divisor = neighbor_norms[None, :] + 1e-05
    keep_factor = keep_mask[0].astype(jnp.float32)
    weight_real = keep_factor * correlation_real.T / divisor
    weight_imag = keep_factor * correlation_imag.T / divisor
    cos_part = jnp.einsum("ij,jgc->igc", weight_real, neighbor, precision=precise)
    sin_part = jnp.einsum("ij,jgc->igc", weight_imag, neighbor, precision=precise)
    new_lower = (lower_edge - combine_halves(cos_part, sin_part)).astype(jnp.bfloat16)
    ortho = jnp.concatenate([new_lower, wavefunctions[EDGE:]], axis=0)
    inverse = (
        jnp.zeros((sticks_dev,), jnp.int32)
        .at[stick_map]
        .set(jnp.arange(sticks_dev, dtype=jnp.int32))
    )
    freq_block = jnp.take(ortho, inverse, axis=1).reshape(bands_dev, GBOX, rows_local, row_width)
    ahead_cos, ahead_sin, behind_cos, behind_sin = dft_tables(GBOX, GRID)
    ahead_last = last_matrix(ahead_cos, ahead_sin)
    behind_last = last_matrix(behind_cos, behind_sin)
    doubled = jnp.concatenate([potential, potential], axis=-1)
    section_one = along_axis(freq_block, ahead_cos, ahead_sin, "bkyc,kn->bnyc").astype(jnp.bfloat16)
    section_two = along_last(
        lax.all_to_all(section_one, "pencil", split_axis=1, concat_axis=2, tiled=True), ahead_last
    ).astype(jnp.bfloat16)
    real_space = along_axis(section_two, ahead_cos, ahead_sin, "bxkc,kn->bxnc").astype(jnp.bfloat16)
    scaled = (doubled * real_space.astype(jnp.float32)).astype(jnp.bfloat16)
    back_one = along_axis(scaled, behind_cos, behind_sin, "bxnc,nk->bxkc").astype(jnp.bfloat16)
    back_two = along_last(back_one, behind_last).astype(jnp.bfloat16)
    back_two = lax.all_to_all(back_two, "pencil", split_axis=2, concat_axis=1, tiled=True)
    back_three = along_axis(back_two, behind_cos, behind_sin, "bnyc,nk->bkyc")
    row_start = lax.axis_index("pencil") * rows_local
    kinetic = kinetic_table(GBOX, row_start, rows_local)
    result = (back_three + kinetic * freq_block.astype(jnp.float32)).astype(jnp.bfloat16)
    result = result.reshape(bands_dev, sticks_dev, row_width)
    return jnp.take(result, stick_map, axis=1)


def solution(mesh):
    return jax.shard_map(
        local,
        mesh=mesh,
        in_specs=(
            P("cuts", "pencil", None),
            P("pencil", None, None),
            P("cuts", None, None),
            P("pencil"),
        ),
        out_specs=P("cuts", "pencil", None),
        check_vma=False,
    )
```

profile of v0, /device:TPU:4, one launch (start us, length us, event | category | flops | bytes accessed | tf_op | source)
XLA Modules:
  0.0 940.4 jit_solution(16754301798548629606)
XLA Ops:
  0.0 3.6 fusion.100
  3.6 3.1 copy.68
  9.8 9.7 %scatter_custom_fusion = s32[2304]{0:T(1024)S(1)} fusion(s32[2304]{0:T(1024)} %compare_select_fusion, s32[2304]{0:T(1024)} %iota.60, s32[]{:T(128)} %constant.27.clone.1), kind=kCustom, calls=%fused_computation.98 | custom fusion | bytes 9728 | tf_op jit(solution)/shard_map/scatter | solution.py:98
  20.8 10.9 %collective-permute-done = bf16[2,2304,192]{1,0,2:T(2,128)(2,1)} collective-permute-done((bf16[2,2304,192]{1,0,2:T(2,128)(2,1)}, bf16[2,2304,192]{1,0,2:T(2,128)(2,1)}, u32[]{:S(2)}, u32[]{:S(2)}) %collective-permute-start) | collective-permute-done | bytes 1769504 | tf_op jit(solution)/shard_map/ppermute | solution.py:16
  31.7 5.2 multiply_reduce_fusion
  36.9 3.2 convolution_bitcast_fusion.6
  40.2 7.3 convolution_bitcast_fusion.8
  47.5 3.3 fusion.16
  50.8 12.1 %all-reduce = (f32[2,2]{1,0:T(2,128)S(1)}, f32[2]{0:T(128)S(1)}, f32[2,2]{1,0:T(2,128)S(1)}) all-reduce(f32[2,2]{1,0:T(2,128)S(1)} %convolution_bitcast_fusion.8, f32[2]{0:T(128)S(1)} %multiply_reduce_fusion, f32[2,2]{1,0:T(2,128)S(1)} %fusion.16), channel_id=1, replica_groups=mesh['cuts'=8,'pencil'=4] {'pencil'}, use_global_device_ids=true, to_apply=%region_0.0 | all-reduce | flops 10 | bytes 80 | tf_op jit(solution)/shard_map/psum | solution.py:84
  62.9 7.0 fusion.56
  69.9 7.2 fusion.58
  81.3 5.1 pad_maximum_fusion.2
  86.4 7.1 copy.38
  93.5 13.0 %gather_fusion = bf16[2304,4,192]{2,1,0:T(4,128)(2,1)} fusion(bf16[4,2304,192]{2,0,1:T(4,128)(2,1)} %copy.38, s32[3072]{0:T(1024)S(1)} %copy-done.6), kind=kCustom, calls=%fused_computation.clone | custom fusion | bytes 7087104 | tf_op jit(solution)/shard_map/jit(_take)/gather | solution.py:100
  106.5 9.5 %select_bitcast_fusion.1 = bf16[4,2304,192]{2,0,1:T(4,128)(2,1)S(1)} fusion(bf16[2304,4,192]{2,1,0:T(4,128)(2,1)} %gather_fusion, pred[2304]{0:T(1024)(128)(4,1)S(1)} %copy-done.13), kind=kLoop, calls=%fused_computation.33 | loop fusion | flops 1769472 | bytes 7080192 | tf_op jit(solution)/shard_map/jit(_take)/select_n | solution.py:100
  116.1 2.8 copy.39
  118.8 7.3 copy.40
  126.2 5.7 fusion.49
  131.8 8.3 fusion.47
  140.1 12.3 %fusion.9 = (bf16[4,192,24,96]{1,3,2,0:T(8,128)(2,1)}, bf16[4,192,24,96]{1,3,2,0:T(8,128)(2,1)}) fusion(f32[4,192,24,192]{1,3,2,0:T(8,128)} %bitcast.114, f32[4,192,24,192]{1,3,2,0:T(8,128)S(1)} %bitcast.113), kind=kLoop, calls=%fused_computation.25 | loop fusion | flops 7077888 | bytes 35389440 | tf_op jit(solution)/shard_map/convert.4
  152.5 9.5 %pad_maximum_fusion.1 = bf16[4,192,24,192]{1,3,2,0:T(8,128)(2,1)} fusion(bf16[4,192,24,96]{1,3,2,0:T(8,128)(2,1)} %get-tuple-element.14, bf16[4,192,24,96]{1,3,2,0:T(8,128)(2,1)} %get-tuple-element.13), kind=kLoop, calls=%fused_computation.26 | loop fusion | flops 14155776 | bytes 14155776 | tf_op jit(solution)/shard_map/concatenate | solution.py:42
  162.0 14.0 %copy.42 = bf16[4,192,24,192]{3,2,0,1:T(8,128)(2,1)} copy(bf16[4,192,24,192]{1,3,2,0:T(8,128)(2,1)} %pad_maximum_fusion.1) | data formatting | bytes 14155776 | tf_op jit(solution)/shard_map/concatenate | solution.py:42
  176.0 6.2 all-to-all-start
  185.4 13.5 %pad_maximum_fusion = f32[48,192,384]{2,1,0:T(8,128)} fusion(f32[48,192,192]{2,1,0:T(8,128)} %param.7), kind=kLoop, calls=%fused_computation.14 | loop fusion | flops 3538944 | bytes 21233664 | tf_op jit(solution)/shard_map/concatenate | solution.py:104
  198.9 185.5 %all-to-all-done = bf16[4,192,24,192]{3,2,0,1:T(8,128)(2,1)} async-done(((bf16[4,192,24,192]{3,2,0,1:T(8,128)(2,1)}), bf16[4,192,24,192]{3,2,0,1:T(8,128)(2,1)}, u32[]{:S(2)}, u32[]{:S(2)}) %all-to-all-start) | async-done | bytes 7077920 | tf_op jit(solution)/shard_map/all_to_all | solution.py:107
  384.4 8.4 copy.44
  392.8 14.6 %convolution_convert_fusion = bf16[4,48,96,384]{3,2,1,0:T(8,128)(2,1)} fusion(bf16[4,48,96,192]{3,2,1,0:T(8,128)(2,1)} %bitcast.121, bf16[96,192]{1,0:T(8,128)(2,1)S(1)} %get-tuple-element.26, bf16[96,192]{1,0:T(8,128)(2,1)S(1)} %fusion.46, bf16[96,192]{1,0:T(8,128)(2,1)S(1)} %get-tuple-element.25), kind=kOutput, calls=%fused_computation.21 | convolution fusion | flops 2725576704 | bytes 21344256 | tf_op jit(solution)/shard_map/bxyc,cd->bxyd/dot_general | solution.py:52
  407.4 24.7 %convolution_bitcast_fusion.1 = f32[4,48,192,384]{3,2,1,0:T(8,128)} fusion(bf16[4,48,96,384]{3,2,1,0:T(8,128)(2,1)} %convolution_convert_fusion, f32[96]{0:T(128)S(1)} %iota_add_fusion), kind=kOutput, calls=%fused_computation.9 | convolution fusion | flops 2718093312 | bytes 70779264 | tf_op jit(solution)/shard_map/bxkc,kn->bxnc/dot_general | solution.py:46
  432.1 24.7 %convolution_bitcast_fusion = f32[4,48,192,384]{3,2,1,0:T(8,128)} fusion(bf16[4,48,96,384]{3,2,1,0:T(8,128)(2,1)} %convolution_convert_fusion, f32[96]{0:T(128)S(1)} %iota_add_fusion), kind=kOutput, calls=%fused_computation.8 | convolution fusion | flops 2718093312 | bytes 70779264 | tf_op jit(solution)/shard_map/bxkc,kn->bxnc/dot_general | solution.py:47
  456.9 61.3 %fusion.1 = (bf16[4,48,192,192]{3,2,1,0:T(8,128)(2,1)}, bf16[4,48,192,192]{3,2,1,0:T(8,128)(2,1)}) fusion(f32[4,48,192,384]{3,2,1,0:T(8,128)} %convolution_bitcast_fusion, f32[4,48,192,384]{3,2,1,0:T(8,128)} %convolution_bitcast_fusion.1), kind=kLoop, calls=%fused_computation.7 | loop fusion | flops 28311552 | bytes 141557760 | tf_op jit(solution)/shard_map/convert.2
  518.2 28.5 %convolution_bitcast_fusion.3 = f32[4,48,96,384]{3,2,1,0:T(8,128)} fusion(bf16[4,48,192,192]{3,2,1,0:T(8,128)(2,1)} %get-tuple-element.10, bf16[4,48,192,192]{3,2,1,0:T(8,128)(2,1)} %get-tuple-element.9, f32[48,192,384]{2,1,0:T(8,128)} %pad_maximum_fusion, f32[96]{0:T(128)S(1)} %iota_add_fusion), kind=kOutput, calls=%fused_computation.20 | convolution fusion | flops 2803027968 | bytes 70779264 | tf_op jit(solution)/shard_map/bxnc,nk->bxkc/dot_general | solution.py:46
  546.7 28.5 %convolution_bitcast_fusion.2 = f32[4,48,96,384]{3,2,1,0:T(8,128)} fusion(bf16[4,48,192,192]{3,2,1,0:T(8,128)(2,1)} %get-tuple-element.10, bf16[4,48,192,192]{3,2,1,0:T(8,128)(2,1)} %get-tuple-element.9, f32[48,192,384]{2,1,0:T(8,128)} %pad_maximum_fusion, f32[96]{0:T(128)S(1)} %iota_add_fusion), kind=kOutput, calls=%fused_computation.19 | convolution fusion | flops 2803046400 | bytes 70779264 | tf_op jit(solution)/shard_map/bxnc,nk->bxkc/dot_general | solution.py:47
  575.2 32.3 %fusion.3 = (bf16[4,48,96,192]{3,2,1,0:T(8,128)(2,1)}, bf16[4,48,96,192]{3,2,1,0:T(8,128)(2,1)}) fusion(f32[4,48,96,384]{3,2,1,0:T(8,128)} %convolution_bitcast_fusion.2, f32[4,48,96,384]{3,2,1,0:T(8,128)} %convolution_bitcast_fusion.3), kind=kLoop, calls=%fused_computation.13 | loop fusion | flops 14155776 | bytes 70778880 | tf_op jit(solution)/shard_map/convert
  607.6 13.8 %fusion.11 = bf16[4,48,96,192]{3,2,1,0:T(8,128)(2,1)} fusion(bf16[4,48,96,192]{3,2,1,0:T(8,128)(2,1)} %get-tuple-element.12, bf16[4,48,96,192]{3,2,1,0:T(8,128)(2,1)} %get-tuple-element.11, bf16[192,96]{0,1:T(8,128)(2,1)S(1)} %copy-done.9, bf16[192,96]{0,1:T(8,128)(2,1)S(1)} %copy-done.7, bf16[192,96]{0,1:T(8,128)(2,1)S(1)} %copy-done.8), kind=kOutput, calls=%fused_computation.29 | convolution fusion | flops 2750349312 | bytes 21344256 | tf_op jit(solution)/shard_map/bxyc,cd->bxyd/dot_general | solution.py:52
  621.3 12.7 %copy.47 = bf16[4,48,96,192]{3,1,0,2:T(8,128)(2,1)} copy(bf16[4,48,96,192]{3,2,1,0:T(8,128)(2,1)} %fusion.11) | data formatting | bytes 14155776 | tf_op jit(solution)/shard_map/convert_element_type | solution.py:112
  634.0 6.3 all-to-all-start.1
  642.5 203.0 %all-to-all-done.1 = bf16[4,48,96,192]{3,1,0,2:T(8,128)(2,1)} async-done(((bf16[4,48,96,192]{3,1,0,2:T(8,128)(2,1)}), bf16[4,48,96,192]{3,1,0,2:T(8,128)(2,1)}, u32[]{:S(2)}, u32[]{:S(2)}) %all-to-all-start.1) | async-done | bytes 7077920 | tf_op jit(solution)/shard_map/all_to_all | solution.py:113
  845.4 8.7 copy.48
  854.2 5.6 convolution_bitcast_fusion.5
  862.4 5.0 slice_subtract_fusion.3
  867.4 5.2 copy.49
  872.7 10.2 %copy.51 = f32[4,2304,96]{2,0,1:T(4,128)S(1)} copy(f32[4,2304,96]{2,1,0:T(8,128)S(1)} %bitcast.125) | data formatting | bytes 7077888 | tf_op jit(solution)/shard_map/concatenate | solution.py:42
  883.0 2.7 copy.50
  885.7 10.1 %copy.52 = f32[4,2304,96]{2,0,1:T(4,128)S(1)} copy(f32[4,2304,96]{2,1,0:T(8,128)S(1)} %bitcast.126) | data formatting | bytes 7077888 | tf_op jit(solution)/shard_map/concatenate | solution.py:42
  895.9 13.1 %fusion.10 = bf16[4,2304,192]{2,0,1:T(4,128)(2,1)} fusion(f32[4,2304,96]{2,0,1:T(4,128)S(1)} %copy.52, f32[4,2304,96]{2,0,1:T(4,128)S(1)} %copy.51, f32[2304,192]{1,0:T(8,128)S(1)} %copy-done.2, bf16[2304,4,192]{2,1,0:T(4,128)(2,1)S(1)} %bitcast.120, pred[2304]{0:T(1024)(128)(4,1)S(1)} %copy-done.14), kind=kLoop, calls=%fused_computation.28 | loop fusion | flops 10616832 | bytes 15927552 | tf_op jit(solution)/shard_map/convert_element_type | solution.py:117
  909.0 13.0 %gather_fusion.1 = bf16[2304,4,192]{2,1,0:T(4,128)(2,1)} fusion(bf16[4,2304,192]{2,0,1:T(4,128)(2,1)} %fusion.10, s32[3072]{0:T(1024)S(1)} %pad_clamp_fusion), kind=kCustom, calls=%fused_computation.1.clone | custom fusion | bytes 7087104 | tf_op jit(solution)/shard_map/jit(_take)/gather | solution.py:119
  922.0 10.2 %select_bitcast_fusion = bf16[4,2304,192]{2,0,1:T(4,128)(2,1)} fusion(bf16[2304,4,192]{2,1,0:T(4,128)(2,1)} %gather_fusion.1, pred[2304]{0:T(1024)(128)(4,1)S(1)} %compare_and_fusion), kind=kLoop, calls=%fused_computation.32 | loop fusion | flops 1769472 | bytes 7080192 | tf_op jit(solution)/shard_map/jit(_take)/select_n | solution.py:119
  932.2 8.1 copy.53
  (66 shorter events, 16.5 us)
Async XLA Ops:
  0.0 20.7 %copy-start.3 = (bf16[4,2304,192]{1,2,0:T(8,128)(2,1)S(1)}, bf16[4,2304,192]{1,2,0:T(8,128)(2,1)}, u32[]{:S(2)}) copy-start(bf16[4,2304,192]{1,2,0:T(8,128)(2,1)} %param.6) | copy-start | bytes 10616836
  0.0 8.6 copy-start.11
  6.7 25.0 %collective-permute-start = (bf16[2,2304,192]{1,0,2:T(2,128)(2,1)}, bf16[2,2304,192]{1,0,2:T(2,128)(2,1)}, u32[]{:S(2)}, u32[]{:S(2)}) collective-permute-start(bf16[2,2304,192]{1,0,2:T(2,128)(2,1)} %copy.68), channel_id=1, source_target_pairs={{0,4},{4,8},{8,12},{12,16},{16,20},{20,24},{24,28},{1,5},{5,9},{9,... | collective-permute-start | bytes 5308424 | tf_op jit(solution)/shard_map/ppermute | solution.py:16
  19.5 20.7 %copy-start.4 = (bf16[2,2304,192]{1,2,0:T(8,128)(2,1)S(1)}, bf16[2,2304,192]{1,2,0:T(8,128)(2,1)}, u32[]{:S(2)}) copy-start(bf16[2,2304,192]{1,2,0:T(8,128)(2,1)} %get-tuple-element.21) | copy-start | bytes 5308420
  40.2 22.7 %copy-start.15 = (s32[1,2,2]{2,1,0:T(2,128)S(1)}, s32[1,2,2]{2,1,0:T(2,128)}, u32[]{:S(2)}) copy-start(s32[1,2,2]{2,1,0:T(2,128)} %param.8) | copy-start | bytes 52
  69.9 9.1 copy-start.5
  81.3 12.2 %copy-start.6 = (s32[3072]{0:T(1024)S(1)}, s32[3072]{0:T(1024)}, u32[]{:S(2)}) copy-start(s32[3072]{0:T(1024)} %pad_clamp_fusion.1) | copy-start | bytes 36868
  93.5 13.0 %copy-start.13 = (pred[2304]{0:T(1024)(128)(4,1)S(1)}, pred[2304]{0:T(1024)(128)(4,1)}, u32[]{:S(2)}) copy-start(pred[2304]{0:T(1024)(128)(4,1)} %compare_and_fusion.1) | copy-start | bytes 6916
  126.2 5.7 copy-start.1
  176.0 208.4 %all-to-all-start = ((bf16[4,192,24,192]{3,2,0,1:T(8,128)(2,1)}), bf16[4,192,24,192]{3,2,0,1:T(8,128)(2,1)}, u32[]{:S(2)}, u32[]{:S(2)}) async-start(bf16[4,192,24,192]{3,2,0,1:T(8,128)(2,1)} %copy.42), calls=%async_computation | async-start | bytes 18874368 | tf_op jit(solution)/shard_map/all_to_all | solution.py:107
  575.2 32.3 %copy-start.7 = (bf16[192,96]{0,1:T(8,128)(2,1)S(1)}, bf16[192,96]{0,1:T(8,128)(2,1)}, u32[]{:S(2)}) copy-start(bf16[192,96]{0,1:T(8,128)(2,1)} %fusion.48) | copy-start | bytes 110596
  575.2 32.3 %copy-start.8 = (bf16[192,96]{0,1:T(8,128)(2,1)S(1)}, bf16[192,96]{0,1:T(8,128)(2,1)}, u32[]{:S(2)}) copy-start(bf16[192,96]{0,1:T(8,128)(2,1)} %get-tuple-element.23) | copy-start | bytes 110596
  575.2 32.3 %copy-start.9 = (bf16[192,96]{0,1:T(8,128)(2,1)S(1)}, bf16[192,96]{0,1:T(8,128)(2,1)}, u32[]{:S(2)}) copy-start(bf16[192,96]{0,1:T(8,128)(2,1)} %get-tuple-element.24) | copy-start | bytes 110596
  634.0 6.6 copy-start.10
  634.0 6.7 copy-start.12
  634.0 211.4 %all-to-all-start.1 = ((bf16[4,48,96,192]{3,1,0,2:T(8,128)(2,1)}), bf16[4,48,96,192]{3,1,0,2:T(8,128)(2,1)}, u32[]{:S(2)}, u32[]{:S(2)}) async-start(bf16[4,48,96,192]{3,1,0,2:T(8,128)(2,1)} %copy.47), calls=%async_computation.1 | async-start | bytes 18874368 | tf_op jit(solution)/shard_map/all_to_all | solution.py:113
  854.2 6.4 copy-start
  867.4 15.5 %slice-start.2 = ((s8[4718592]{0:T(1024)(128)(4,1)}), s8[4194304]{0:T(1024)(128)(4,1)S(1)}, s32[]{:S(2)}) async-start(s8[4718592]{0:T(1024)(128)(4,1)} %bitcast.122), calls=%async_computation.4 | async-start | bytes 8388608
  872.6 10.3 %slice-start.3 = ((s8[4718592]{0:T(1024)(128)(4,1)}), s8[524288]{0:T(1024)(128)(4,1)S(1)}, s32[]{:S(2)}) async-start(s8[4718592]{0:T(1024)(128)(4,1)} %bitcast.122), calls=%async_computation.5 | async-start | bytes 1048576
  882.9 12.9 %slice-start = ((s8[4718592]{0:T(1024)(128)(4,1)}), s8[4194304]{0:T(1024)(128)(4,1)S(1)}, s32[]{:S(2)}) async-start(s8[4718592]{0:T(1024)(128)(4,1)} %bitcast.119), calls=%async_computation.2 | async-start | bytes 8388608
  882.9 12.9 %copy-start.2 = (f32[2304,192]{1,0:T(8,128)S(1)}, f32[2304,192]{1,0:T(8,128)}, u32[]{:S(2)}) copy-start(f32[2304,192]{1,0:T(8,128)} %add_multiply_fusion) | copy-start | bytes 5308420
  883.0 12.9 %copy-start.14 = (pred[2304]{0:T(1024)(128)(4,1)S(1)}, pred[2304]{0:T(1024)(128)(4,1)}, u32[]{:S(2)}) copy-start(pred[2304]{0:T(1024)(128)(4,1)} %compare_and_fusion.1) | copy-start | bytes 6916
  885.7 10.1 %slice-start.1 = ((s8[4718592]{0:T(1024)(128)(4,1)}), s8[524288]{0:T(1024)(128)(4,1)S(1)}, s32[]{:S(2)}) async-start(s8[4718592]{0:T(1024)(128)(4,1)} %bitcast.119), calls=%async_computation.3 | async-start | bytes 1048576
where the time goes:
time: 945 us; the launch traced here: 940 us
  waiting for transfers between devices  399 us (42%)
  other arithmetic  188 us (20%)
  matrix products  184 us (19%)
  local copies, waits for them, and re-layouts  141 us (15%)
  starting transfers between devices  14.5 us (2%)
  blocking collectives  12.1 us (1%)
    all_to_all x1, waiting for transfers between devices, local(): lax.all_to_all(back_two, 'pencil', split_axis=2, concat_axis=1, tiled=True)  203 us
    all_to_all x1, waiting for transfers between devices, local(): lax.all_to_all(section_one, 'pencil', split_axis=1, concat_axis=2, tiled=...  185 us
    another operation x3, other arithmetic  106 us
    dot_general x3, matrix products, along_axis(): jnp.einsum(pattern, values, cos_table, preferred_element_type=jnp.float32)  58.9 us
    dot_general x3, matrix products, along_axis(): jnp.einsum(pattern, values, sin_table, preferred_element_type=jnp.float32)  55.1 us
    concatenate x3, local copies, waits for them, and re-layouts, combine_halves(): return jnp.concatenate([real_part, imag_part], axis=-1)  34.3 us
    dot_general x2, matrix products, along_last(): jnp.einsum('bxyc,cd->bxyd', values, matrix, preferred_element_type=jnp.fl...  28.3 us
  transfers between devices with their start and end apart: 3, of which 3 were waited for; matrix products, arithmetic and copies ran while one was open for 3% of the time, Pallas kernels for 0%

commit v1 on v0

v1 whole, which is shorter than its diff:
```python
import math

import jax
import jax.numpy as jnp
import numpy as np
from jax import lax
from jax.experimental import pallas as pl
from jax.experimental.pallas import tpu as pltpu
from jax.sharding import PartitionSpec as P

EDGE = 2
VMEM_BYTES = 56 * 1024 * 1024
F32 = jnp.float32
BF16 = jnp.bfloat16


def from_behind(block, axis, distance):
    devices = range(lax.axis_size(axis))
    route = [(i - distance, i) for i in devices if i - distance in devices]
    return lax.ppermute(block, axis, route)


def dft_tables(box_size, length):
    frequency = np.arange(box_size) - box_size // 2
    points = np.arange(length)
    phases = 2.0 * math.pi / length * np.mod(frequency[:, None] * points[None, :], length)
    ahead_scale = 1.0 / math.sqrt(box_size)
    behind_scale = math.sqrt(box_size) / length
    ahead_cos = np.cos(phases) * ahead_scale
    ahead_sin = np.sin(phases) * ahead_scale
    behind_cos = np.cos(phases).T * behind_scale
    behind_sin = -np.sin(phases).T * behind_scale
    return tuple(
        jnp.asarray(t.astype(np.float32)).astype(BF16)
        for t in (ahead_cos, ahead_sin, behind_cos, behind_sin)
    )


def last_matrix(cos_table, sin_table):
    upper_rows = jnp.concatenate([cos_table, sin_table], axis=1)
    lower_rows = jnp.concatenate([-sin_table, cos_table], axis=1)
    return jnp.concatenate([upper_rows, lower_rows], axis=0)


def combine_halves(cos_part, sin_part):
    middle = cos_part.shape[-1] // 2
    real_part = cos_part[..., :middle] - sin_part[..., middle:]
    imag_part = sin_part[..., :middle] + cos_part[..., middle:]
    return jnp.concatenate([real_part, imag_part], axis=-1)


def along_axis(values, cos_table, sin_table, pattern):
    cos_part = jnp.einsum(pattern, values, cos_table, preferred_element_type=F32)
    sin_part = jnp.einsum(pattern, values, sin_table, preferred_element_type=F32)
    return combine_halves(cos_part, sin_part)


def along_last(values, matrix):
    return jnp.einsum("bxyc,cd->bxyd", values, matrix, preferred_element_type=F32)


def kinetic_table(box_size, row_start, column_count):
    center = box_size // 2
    freq_rows = jnp.arange(box_size, dtype=F32) - center
    freq_cols = (row_start + jnp.arange(column_count, dtype=jnp.int32)).astype(F32) - center
    freq_depth = jnp.arange(box_size, dtype=F32) - center
    freq_depth = jnp.concatenate([freq_depth, freq_depth])
    squares = (
        freq_rows[:, None, None] ** 2
        + freq_cols[None, :, None] ** 2
        + freq_depth[None, None, :] ** 2
    )
    return 0.5 * squares / float(center * center)


def turned(values):
    middle = values.shape[-1] // 2
    return jnp.concatenate([-values[..., middle:], values[..., :middle]], axis=-1)


def turned_rows(values):
    middle = values.shape[0] // 2
    return jnp.concatenate([-values[middle:], values[:middle]], axis=0)


def lane_block(count, parts):
    block = count // parts
    return block if count % parts == 0 and block % 128 == 0 else count


def dot(a, b):
    return jnp.dot(a, b, preferred_element_type=F32)


def params(grid_dims=1):
    return pltpu.CompilerParams(
        dimension_semantics=("arbitrary",) * grid_dims, vmem_limit_bytes=VMEM_BYTES
    )


def edge_sums_kernel(behind_ref, own_ref, out_ref):
    @pl.when(pl.program_id(0) == 0)
    def _():
        out_ref[...] = jnp.zeros_like(out_ref)

    def add(slot, values):
        rows, width = values.shape
        out_ref[slot] += jnp.sum(values.reshape(rows // 8, 8, width), axis=0)

    own = [own_ref[i].astype(F32) for i in range(EDGE)]
    for j in range(EDGE):
        behind = behind_ref[j].astype(F32)
        swapped = turned_rows(behind)
        for i in range(EDGE):
            add(j * EDGE + i, behind * own[i])
            add(EDGE * EDGE + j * EDGE + i, swapped * own[i])
        add(2 * EDGE * EDGE + j, behind * behind)


def edge_sums(neighbor, bands):
    edge, row_width, sticks_dev = neighbor.shape
    width = lane_block(sticks_dev, 6)
    slots = 2 * EDGE * EDGE + EDGE
    sums = pl.pallas_call(
        edge_sums_kernel,
        grid=(sticks_dev // width,),
        in_specs=[
            pl.BlockSpec((edge, row_width, width), lambda g: (0, 0, g)),
            pl.BlockSpec((edge, row_width, width), lambda g: (0, 0, g)),
        ],
        out_specs=pl.BlockSpec((slots, 8, width), lambda g: (0, 0, 0)),
        out_shape=jax.ShapeDtypeStruct((slots, 8, width), F32),
        compiler_params=params(),
    )(neighbor, bands)
    return jnp.sum(sums, axis=(1, 2))


def edge_weights(sums, keep_mask):
    count = EDGE * EDGE
    real = sums[:count].reshape(EDGE, EDGE)
    imag = sums[count : 2 * count].reshape(EDGE, EDGE)
    divisor = sums[2 * count :][None, :] + 1e-05
    keep = keep_mask[0].astype(F32)
    return jnp.stack([keep * real.T / divisor, keep * imag.T / divisor]).reshape(-1)


def place_kernel(weight_ref, place_ref, own_ref, behind_ref, out_ref, ortho):
    bands, _, sticks_dev = own_ref.shape
    rows = out_ref.shape[1]
    chunk = lane_block(sticks_dev, 9)
    step = pl.program_id(0)

    @pl.when(step == 0)
    def _():
        ortho[EDGE:] = own_ref[EDGE:]

        @pl.loop(0, sticks_dev // chunk)
        def _(c):
            part = pl.ds(pl.multiple_of(c * chunk, chunk), chunk)
            behind = [behind_ref[j, :, part].astype(F32) for j in range(EDGE)]
            swapped = [turned_rows(values) for values in behind]
            for i in range(EDGE):
                total = own_ref[i, :, part].astype(F32)
                for j in range(EDGE):
                    total -= weight_ref[i * EDGE + j] * behind[j]
                    total -= weight_ref[EDGE * EDGE + i * EDGE + j] * swapped[j]
                ortho[i, :, part] = total.astype(BF16)

    position = step * rows + lax.broadcasted_iota(jnp.int32, (rows, sticks_dev), 0)
    chosen = jnp.where(position == place_ref[...], 1.0, 0.0).astype(BF16)
    for b in range(bands):
        out_ref[b] = lax.dot_general(
            chosen, ortho[b], (((1,), (1,)), ((), ())), preferred_element_type=F32
        ).astype(BF16)


def place(weights, places, own, neighbor):
    bands, row_width, sticks_dev = own.shape
    steps = 4
    rows = sticks_dev // steps
    whole = lambda shape: pl.BlockSpec(shape, lambda g: (0,) * len(shape))
    return pl.pallas_call(
        place_kernel,
        grid=(steps,),
        in_specs=[
            pl.BlockSpec(memory_space=pltpu.SMEM),
            whole((1, sticks_dev)),
            whole(own.shape),
            whole(neighbor.shape),
        ],
        out_specs=pl.BlockSpec((bands, rows, row_width), lambda g: (0, g, 0)),
        out_shape=jax.ShapeDtypeStruct((bands, sticks_dev, row_width), BF16),
        scratch_shapes=[pltpu.VMEM(own.shape, BF16)],
        compiler_params=params(),
    )(weights, places.reshape(1, sticks_dev), own, neighbor)


def unplace_kernel(place_ref, rows_ref, out_ref, columns):
    bands, sticks_dev, row_width = rows_ref.shape

    @pl.when(pl.program_id(0) == 0)
    def _():
        for b in range(bands):
            columns[b * row_width : (b + 1) * row_width] = rows_ref[b].T

    width = out_ref.shape[2]
    position = lax.broadcasted_iota(jnp.int32, (sticks_dev, width), 0)
    chosen = jnp.where(position == place_ref[...], 1.0, 0.0).astype(BF16)
    result = dot(columns[...], chosen).astype(BF16)
    for b in range(bands):
        out_ref[b] = result[b * row_width : (b + 1) * row_width]


def unplace(places, values):
    bands, sticks_dev, row_width = values.shape
    width = lane_block(sticks_dev, 3)
    return pl.pallas_call(
        unplace_kernel,
        grid=(sticks_dev // width,),
        in_specs=[
            pl.BlockSpec((1, width), lambda g: (0, g)),
            pl.BlockSpec(values.shape, lambda g: (0, 0, 0)),
        ],
        out_specs=pl.BlockSpec((bands, row_width, width), lambda g: (0, 0, g)),
        out_shape=jax.ShapeDtypeStruct((bands, row_width, sticks_dev), BF16),
        scratch_shapes=[pltpu.VMEM((bands * row_width, sticks_dev), BF16)],
        compiler_params=params(),
    )(places.reshape(1, sticks_dev), values)


def first_ahead_kernel(matrix_ref, in_ref, out_ref):
    for i in range(in_ref.shape[0]):
        values = in_ref[i]
        stacked = jnp.concatenate([values, turned(values)], axis=0)
        out_ref[i] = dot(matrix_ref[...], stacked).astype(BF16)


def first_ahead(matrix, block):
    columns, box_size, row_width = block.shape
    length = matrix.shape[0]
    per_step = 12 if columns % 12 == 0 else 1
    return pl.pallas_call(
        first_ahead_kernel,
        grid=(columns // per_step,),
        in_specs=[
            pl.BlockSpec(matrix.shape, lambda g: (0, 0)),
            pl.BlockSpec((per_step, box_size, row_width), lambda g: (g, 0, 0)),
        ],
        out_specs=pl.BlockSpec((per_step, length, row_width), lambda g: (g, 0, 0)),
        out_shape=jax.ShapeDtypeStruct((columns, length, row_width), BF16),
        compiler_params=params(),
    )(matrix, block)


def first_behind_kernel(matrix_ref, in_ref, freq_ref, out_ref):
    per_step, box_size, row_width = freq_ref.shape
    center = box_size // 2
    shape = (box_size, row_width)
    gx = lax.broadcasted_iota(jnp.int32, shape, 0) - center
    gz = lax.broadcasted_iota(jnp.int32, shape, 1)
    gz = jnp.where(gz >= box_size, gz - box_size, gz) - center
    scale = 0.5 / float(center * center)
    squares = (gx * gx + gz * gz).astype(F32)
    for i in range(per_step):
        values = in_ref[i]
        stacked = jnp.concatenate([values, turned(values)], axis=0)
        gy = pl.program_id(0) * per_step + i - center
        kinetic = (squares + (gy * gy).astype(F32)) * scale
        total = dot(matrix_ref[...], stacked) + kinetic * freq_ref[i].astype(F32)
        out_ref[i] = total.astype(BF16)


def first_behind(matrix, block, freq):
    columns, length, row_width = block.shape
    box_size = matrix.shape[0]
    per_step = 12 if columns % 12 == 0 else 1
    return pl.pallas_call(
        first_behind_kernel,
        grid=(columns // per_step,),
        in_specs=[
            pl.BlockSpec(matrix.shape, lambda g: (0, 0)),
            pl.BlockSpec((per_step, length, row_width), lambda g: (g, 0, 0)),
            pl.BlockSpec((per_step, box_size, row_width), lambda g: (g, 0, 0)),
        ],
        out_specs=pl.BlockSpec((per_step, box_size, row_width), lambda g: (g, 0, 0)),
        out_shape=jax.ShapeDtypeStruct((columns, box_size, row_width), BF16),
        compiler_params=params(),
    )(matrix, block, freq)


def planes_kernel(last_re, last_im, mid_ahead, mid_behind, back_re, back_im, in_ref, pot_ref, out_ref):
    planes, box_size, row_width = in_ref.shape
    length = pot_ref.shape[-1]
    rows = in_ref[...].reshape(planes * box_size, row_width)
    real = dot(rows, last_re[...]).astype(BF16)
    imag = dot(rows, last_im[...]).astype(BF16)
    for i in range(planes):
        part = slice(i * box_size, (i + 1) * box_size)
        stacked = jnp.concatenate([real[part], imag[part]], axis=0)
        space = dot(mid_ahead[...], stacked)
        local = pot_ref[0, 0, i].astype(F32)
        scaled = jnp.concatenate(
            [(space[:length] * local).astype(BF16), (space[length:] * local).astype(BF16)], axis=0
        )
        back = dot(mid_behind[...], scaled).astype(BF16)
        out = dot(back[:box_size], back_re[...]) + dot(back[box_size:], back_im[...])
        out_ref[i] = out.astype(BF16)


def planes(matrices, block, potential):
    count, box_size, row_width = block.shape
    cuts, pencils, per_step, length, _ = potential.shape
    return pl.pallas_call(
        planes_kernel,
        grid=(count // per_step,),
        in_specs=[pl.BlockSpec(m.shape, lambda g: (0, 0)) for m in matrices]
        + [
            pl.BlockSpec((per_step, box_size, row_width), lambda g: (g, 0, 0)),
            pl.BlockSpec(
                (1, 1, per_step, length, length), lambda g: (g % cuts, g // cuts, 0, 0, 0)
            ),
        ],
        out_specs=pl.BlockSpec((per_step, box_size, row_width), lambda g: (g, 0, 0)),
        out_shape=jax.ShapeDtypeStruct(block.shape, BF16),
        compiler_params=params(),
    )(*matrices, block, potential)


def hamiltonian_whole_bands(freq_rows, potential_all, rows_local):
    bands_dev, sticks_dev, row_width = freq_rows.shape
    box_size = row_width // 2
    length = potential_all.shape[-1]
    ahead_cos, ahead_sin, behind_cos, behind_sin = dft_tables(box_size, length)
    last_ahead = last_matrix(ahead_cos, ahead_sin)
    last_behind = last_matrix(behind_cos, behind_sin)
    middle_ahead = jnp.concatenate(
        [
            jnp.concatenate([ahead_cos.T, -ahead_sin.T], axis=1),
            jnp.concatenate([ahead_sin.T, ahead_cos.T], axis=1),
        ],
        axis=0,
    )
    middle_behind = jnp.concatenate(
        [
            jnp.concatenate([behind_cos.T, -behind_sin.T], axis=1),
            jnp.concatenate([behind_sin.T, behind_cos.T], axis=1),
        ],
        axis=0,
    )
    first_a = jnp.concatenate([ahead_cos.T, ahead_sin.T], axis=1)
    first_b = jnp.concatenate([behind_cos.T, behind_sin.T], axis=1)
    matrices = (
        last_ahead[:, :length],
        last_ahead[:, length:],
        middle_ahead,
        middle_behind,
        last_behind[:length],
        last_behind[length:],
    )
    sent = freq_rows.reshape(bands_dev, rows_local, box_size, row_width)
    freq = lax.all_to_all(sent, "pencil", split_axis=0, concat_axis=0, tiled=True)
    freq = freq.reshape(bands_dev * rows_local, box_size, row_width)
    section = jnp.swapaxes(first_ahead(first_a, freq), 0, 1)
    section = planes(matrices, section, potential_all)
    result = first_behind(first_b, jnp.swapaxes(section, 0, 1), freq)
    result = result.reshape(bands_dev, rows_local, box_size, row_width)
    result = lax.all_to_all(result, "pencil", split_axis=0, concat_axis=0, tiled=True)
    return result.reshape(bands_dev, sticks_dev, row_width)


def hamiltonian_split_bands(freq_rows, potential, rows_local):
    bands_dev, sticks_dev, row_width = freq_rows.shape
    box_size = row_width // 2
    length = potential.shape[-1]
    freq_block = jnp.swapaxes(freq_rows.reshape(bands_dev, rows_local, box_size, row_width), 1, 2)
    ahead_cos, ahead_sin, behind_cos, behind_sin = dft_tables(box_size, length)
    ahead_last = last_matrix(ahead_cos, ahead_sin)
    behind_last = last_matrix(behind_cos, behind_sin)
    doubled = jnp.concatenate([potential, potential], axis=-1)
    section_one = along_axis(freq_block, ahead_cos, ahead_sin, "bkyc,kn->bnyc").astype(BF16)
    section_two = along_last(
        lax.all_to_all(section_one, "pencil", split_axis=1, concat_axis=2, tiled=True), ahead_last
    ).astype(BF16)
    real_space = along_axis(section_two, ahead_cos, ahead_sin, "bxkc,kn->bxnc").astype(BF16)
    scaled = (doubled * real_space.astype(F32)).astype(BF16)
    back_one = along_axis(scaled, behind_cos, behind_sin, "bxnc,nk->bxkc").astype(BF16)
    back_two = along_last(back_one, behind_last).astype(BF16)
    back_two = lax.all_to_all(back_two, "pencil", split_axis=2, concat_axis=1, tiled=True)
    back_three = along_axis(back_two, behind_cos, behind_sin, "bnyc,nk->bkyc")
    row_start = lax.axis_index("pencil") * rows_local
    kinetic = kinetic_table(box_size, row_start, rows_local)
    result = (back_three + kinetic * freq_block.astype(F32)).astype(BF16)
    return jnp.swapaxes(result, 1, 2).reshape(bands_dev, sticks_dev, row_width)


def local(wavefunctions, potential, keep_mask, stick_map):
    bands_dev, sticks_dev, row_width = wavefunctions.shape
    box_size = row_width // 2
    rows_local = sticks_dev // box_size
    cuts, pencils = lax.axis_size("cuts"), lax.axis_size("pencil")
    whole_bands = bands_dev == pencils and potential.shape[0] % cuts == 0
    if whole_bands:
        share = potential.shape[0] // cuts
        mine = lax.dynamic_slice_in_dim(potential, lax.axis_index("cuts") * share, share, 0)
        potential_all = lax.all_gather(mine.astype(BF16), ("cuts", "pencil"), axis=0, tiled=False)
        potential_all = potential_all.reshape((cuts, pencils) + mine.shape)
    own = jnp.swapaxes(wavefunctions, 1, 2)
    neighbor = from_behind(own[bands_dev - EDGE :], "cuts", 1)
    sums = lax.psum(edge_sums(neighbor, own), "pencil")
    weights = edge_weights(sums, keep_mask)
    places = (stick_map % rows_local) * box_size + stick_map // rows_local
    freq_rows = place(weights, places, own, neighbor)
    if whole_bands:
        result = hamiltonian_whole_bands(freq_rows, potential_all, rows_local)
    else:
        result = hamiltonian_split_bands(freq_rows, potential, rows_local)
    return jnp.swapaxes(unplace(places, result), 1, 2)


def solution(mesh):
    return jax.shard_map(
        local,
        mesh=mesh,
        in_specs=(
            P("cuts", "pencil", None),
            P("pencil", None, None),
            P("cuts", None, None),
            P("pencil"),
        ),
        out_specs=P("cuts", "pencil", None),
        check_vma=False,
    )
```

time: 945 us -> 494 us (0.52)
  waiting for transfers between devices: 399 us -> 27 us
  blocking collectives: 12.1 us -> 278 us
  other arithmetic: 188 us -> 1.16 us
  matrix products: 184 us -> 0 us
  Pallas kernels: 0 us -> 139 us
  local copies, waits for them, and re-layouts: 141 us -> 32.1 us
  between operations: 0.56 us -> 13.4 us
  starting transfers between devices: 14.5 us -> 1.92 us
    all_to_all x2 -> x0, waiting for transfers between devices: 388 us -> none  [the longest x1 203 us: local(): lax.all_to_all(back_two, 'pencil', split_axis=2, concat_axis=1, tiled=True)]
    all_to_all x0 -> x2, blocking collectives: none -> 266 us  [the longest x1 157 us: hamiltonian_whole_bands(): lax.all_to_all(sent, 'pencil', split_axis=0, concat_axis=0, tiled=True)]
    dot_general x13 -> x0, matrix products: 170 us -> none  [the longest x3 58.9 us: along_axis(): jnp.einsum(pattern, values, cos_table, preferred_element_type=jnp.float32)]
    pallas_call x0 -> x6, Pallas kernels: none -> 139 us  [the longest x1 83 us: planes(): pl.pallas_call(planes_kernel, grid=(count // per_step,), in_specs=[pl.Blo...]
    another operation x3 -> x2, other arithmetic: 106 us -> 0.01 us  [edge_weights(): jnp.stack([keep * real.T / divisor, keep * imag.T / divisor]).reshape(-1)]
    concatenate x4 -> x0, local copies, waits for them, and re-layouts: 41.4 us -> none  [the longest x3 34.3 us: combine_halves(): return jnp.concatenate([real_part, imag_part], axis=-1)]
    concatenate x3 -> x0, other arithmetic: 28.2 us -> none  [the longest x1 13.5 us: local(): doubled = jnp.concatenate([potential, potential], axis=-1)]
    gather x2 -> x0, local copies, waits for them, and re-layouts: 26 us -> none  [the longest x1 13 us: local(): jnp.take(ortho, inverse, axis=1)]
  transfers between devices with their start and end apart: 3 -> 2, of which waited for: 3 -> 1; matrix products, arithmetic and copies ran while one was open for 3% -> 3% of each run, Pallas kernels for 0% -> 6%
where the time goes in v1:
time: 494 us; the launch traced here: 493 us
  blocking collectives  278 us (56%)
  Pallas kernels  139 us (28%)
  local copies, waits for them, and re-layouts  32.1 us (6%)
  waiting for transfers between devices  27 us (5%)
  between operations  13.4 us (3%)
    all_to_all x1, blocking collectives, hamiltonian_whole_bands(): lax.all_to_all(sent, 'pencil', split_axis=0, concat_axis=0, tiled=True)  157 us
    all_to_all x1, blocking collectives, hamiltonian_whole_bands(): lax.all_to_all(result, 'pencil', split_axis=0, concat_axis=0, tiled=True)  109 us
    pallas_call x1, Pallas kernels, planes(): pl.pallas_call(planes_kernel, grid=(count // per_step,), in_specs=[pl.Blo...  83 us
    ppermute x1, waiting for transfers between devices, from_behind(): return lax.ppermute(block, axis, route)  27 us
    pallas_call x1, Pallas kernels, place(): pl.pallas_call(place_kernel, grid=(steps,), in_specs=[pl.BlockSpec(memory...  17 us
    pallas_call x1, Pallas kernels, unplace(): pl.pallas_call(unplace_kernel, grid=(sticks_dev // width,), in_specs=[pl....  13.4 us
    pallas_call x1, local copies, waits for them, and re-layouts, first_ahead(): pl.pallas_call(first_ahead_kernel, grid=(columns // per_step,), in_specs=...  12.8 us
    pallas_call x1, local copies, waits for them, and re-layouts, planes(): pl.pallas_call(planes_kernel, grid=(count // per_step,), in_specs=[pl.Blo...  12.7 us
  transfers between devices with their start and end apart: 2, of which 1 were waited for; matrix products, arithmetic and copies ran while one was open for 3% of the time, Pallas kernels for 6%

profile of v1, /device:TPU:4, one launch (start us, length us, event | category | flops | bytes accessed | tf_op | source)
XLA Modules:
  0.0 493.5 jit_solution(3325668408063822986)
XLA Ops:
  6.5 0.0 copy-start.1
  6.5 0.0 all-gather.3.cloned.1.call-start
  6.5 2.2 dynamic-slice_convert_fusion
  8.7 0.0 all-gather.3.cloned.1.call-update
  8.7 0.0 copy-start.2
  8.7 1.6 slice.40
  10.3 1.9 collective-permute-start
  12.3 0.0 copy-done.1
  12.3 27.0 %collective-permute-done.behind_ref = bf16[2,192,2304]{2,1,0:T(8,128)(2,1)S(1)} collective-permute-done((bf16[2,192,2304]{2,1,0:T(8,128)(2,1)S(1)}, bf16[2,192,2304]{2,1,0:T(8,128)(2,1)S(1)}, u32[]{:S(2)}, u32[]{:S(2)}) %collective-permute-start) | collective-permute-done | bytes 1769504 | tf_op jit(solution)/shard_map/ppermute | solution.py:20
  39.3 0.0 copy-start
  39.3 1.2 copy-done
  40.5 5.0 %shard_map.82 = f32[10,8,384]{2,1,0:T(8,128)} custom-call(bf16[2,192,2304]{2,1,0:T(8,128)(2,1)} %copy-done, bf16[4,192,2304]{2,1,0:T(8,128)(2,1)} %bitcast.41), custom_call_target="tpu_custom_call" | custom-call | tf_op jit(solution)/shard_map/pallas_call | solution.py:124
  45.5 1.1 reduce_sum.9
  46.5 0.6 reshape.47.place_ref
  47.1 12.4 %psum.7 = f32[10]{0:T(128)S(1)} all-reduce(f32[10]{0:T(128)S(1)} %reduce_sum.9), channel_id=1, replica_groups=mesh['cuts'=8,'pencil'=4] {'pencil'}, use_global_device_ids=true, to_apply=%region_1.0 | all-reduce | flops 10 | bytes 80 | tf_op jit(solution)/shard_map/psum | solution.py:409
  59.5 0.1 fusion.7
  59.6 0.1 reshape.48
  59.7 0.1 copy.13
  59.8 0.1 reshape.49
  59.9 0.1 copy.14
  60.0 0.1 slice_add_fusion
  60.0 0.0 copy-done.2
  60.0 0.6 reshape.50.weight_ref
  60.7 17.0 %shard_map.83 = bf16[4,2304,192]{2,1,0:T(8,128)(2,1)} custom-call(f32[8]{0:T(128)} %reshape.50.weight_ref, s32[1,2304]{1,0:T(1,128)} %reshape.47.place_ref, bf16[4,192,2304]{2,1,0:T(8,128)(2,1)} %bitcast.42, bf16[2,192,2304]{2,1,0:T(8,128)(2,1)} %copy-done), custom_call_target="tpu_custom_call" | custom-call | tf_op jit(solution)/shard_map/pallas_call | solution.py:182
  77.6 157.3 %all_to_all.10 = bf16[4,24,96,192]{3,2,1,0:T(8,128)(2,1)} all-to-all(bf16[4,24,96,192]{3,2,1,0:T(8,128)(2,1)} %bitcast.45), channel_id=1, replica_groups=mesh['cuts'=8,'pencil'=4] {'pencil'}, dimensions={0} | all-to-all | bytes 7077888 | tf_op jit(solution)/shard_map/all_to_all | solution.py:361
  235.0 9.5 %shard_map.84 = bf16[96,192,192]{2,1,0:T(8,128)(2,1)} custom-call(bf16[192,192]{1,0:T(8,128)(2,1)} %constant.77.matrix_ref, bf16[96,96,192]{2,1,0:T(8,128)(2,1)} %bitcast.36), custom_call_target="tpu_custom_call" | custom-call | tf_op jit(solution)/shard_map/pallas_call | solution.py:242
  244.5 12.8 %copy.20 = bf16[96,192,192]{2,0,1:T(8,128)(2,1)} copy(bf16[96,192,192]{2,1,0:T(8,128)(2,1)} %shard_map.84) | data formatting | bytes 14155776 | tf_op jit(solution)/shard_map/pallas_call | solution.py:242
  257.3 0.0 all-gather.3.cloned.1.call-done
  257.3 83.0 %shard_map.85 = bf16[192,96,192]{2,1,0:T(8,128)(2,1)} custom-call(bf16[192,192]{1,0:T(8,128)(2,1)} %constant.62.last_re, bf16[192,192]{1,0:T(8,128)(2,1)} %constant.63.last_im, bf16[384,192]{1,0:T(8,128)(2,1)} %constant.69.mid_ahead, bf16[192,384]{1,0:T(8,128)(2,1)} %constant.73.mid_behind, bf16[192,192]{1,0:T(8,128)(2,1)} %constant.74.back_re, ...), custom_call_target="tpu_custom_call" | custom-call | tf_op jit(solution)/shard_map/pallas_call | solution.py:313
  340.3 12.7 %copy.19 = bf16[192,96,192]{2,0,1:T(8,128)(2,1)} copy(bf16[192,96,192]{2,1,0:T(8,128)(2,1)} %shard_map.85) | data formatting | bytes 14155776 | tf_op jit(solution)/shard_map/pallas_call | solution.py:313
  353.0 11.5 %shard_map.86 = bf16[96,96,192]{2,1,0:T(8,128)(2,1)} custom-call(bf16[96,384]{1,0:T(8,128)(2,1)} %constant.55.matrix_ref, bf16[96,192,192]{2,1,0:T(8,128)(2,1)} %bitcast.38, bf16[96,96,192]{2,1,0:T(8,128)(2,1)} %bitcast.37), custom_call_target="tpu_custom_call" | custom-call | tf_op jit(solution)/shard_map/pallas_call | solution.py:277
  364.5 108.7 %all_to_all.11 = bf16[4,24,96,192]{3,2,1,0:T(8,128)(2,1)} all-to-all(bf16[4,24,96,192]{3,2,1,0:T(8,128)(2,1)} %bitcast.46), channel_id=1, replica_groups=mesh['cuts'=8,'pencil'=4] {'pencil'}, dimensions={0} | all-to-all | bytes 7077888 | tf_op jit(solution)/shard_map/all_to_all | solution.py:367
  473.2 13.4 %shard_map.87 = bf16[4,192,2304]{2,1,0:T(8,128)(2,1)} custom-call(s32[1,2304]{1,0:T(1,128)} %reshape.47.place_ref, bf16[4,2304,192]{2,1,0:T(8,128)(2,1)} %bitcast.43), custom_call_target="tpu_custom_call" | custom-call | tf_op jit(solution)/shard_map/pallas_call | solution.py:217
  (3 shorter events, 0.0 us)
Async XLA Ops:
  6.5 5.7 %copy-start.1 = (s32[2304]{0:T(1024)S(1)}, s32[2304]{0:T(1024)}, u32[]{:S(2)}) copy-start(s32[2304]{0:T(1024)} %param.11) | copy-start | bytes 27652
  6.5 250.7 %all-gather.3.cloned.1.call-start = ((), (), s32[]{:S(2)}) async-start(), calls=%async_computation.2 | async-start | bytes 19464192 | tf_op jit(solution)/shard_map/all_gather | solution.py:405
  8.7 51.3 %copy-start.2 = (s32[1,2,2]{2,1,0:T(2,128)S(1)}, s32[1,2,2]{2,1,0:T(2,128)}, u32[]{:S(2)}) copy-start(s32[1,2,2]{2,1,0:T(2,128)} %param.10) | copy-start | bytes 52
  10.3 29.0 %collective-permute-start = (bf16[2,192,2304]{2,1,0:T(8,128)(2,1)S(1)}, bf16[2,192,2304]{2,1,0:T(8,128)(2,1)S(1)}, u32[]{:S(2)}, u32[]{:S(2)}) collective-permute-start(bf16[2,192,2304]{2,1,0:T(8,128)(2,1)S(1)} %slice.40), channel_id=1, source_target_pairs={{0,4},{4,8},{8,12},{12,16},{16,20},{20,24},{24,28},{1,5},{5,9},{9,... | collective-permute-start | bytes 5308424 | tf_op jit(solution)/shard_map/ppermute | solution.py:20
  39.3 1.2 copy-start
Sparse Core Ops, SparseCore 0:
  10.2 204.1 all-gather.2

commit v2 on v1

--- a/solution.py
+++ b/solution.py
@@ -294,6 +294,7 @@
     rows = in_ref[...].reshape(planes * box_size, row_width)
     real = dot(rows, last_re[...]).astype(BF16)
     imag = dot(rows, last_im[...]).astype(BF16)
+    backs = []
     for i in range(planes):
         part = slice(i * box_size, (i + 1) * box_size)
         stacked = jnp.concatenate([real[part], imag[part]], axis=0)
@@ -303,8 +304,11 @@
             [(space[:length] * local).astype(BF16), (space[length:] * local).astype(BF16)], axis=0
         )
         back = dot(mid_behind[...], scaled).astype(BF16)
-        out = dot(back[:box_size], back_re[...]) + dot(back[box_size:], back_im[...])
-        out_ref[i] = out.astype(BF16)
+        backs.append(back)
+    back_rows = jnp.concatenate([back[:box_size] for back in backs], axis=0)
+    back_turns = jnp.concatenate([back[box_size:] for back in backs], axis=0)
+    out = dot(back_rows, back_re[...]) + dot(back_turns, back_im[...])
+    out_ref[...] = out.astype(BF16).reshape(planes, box_size, row_width)
 
 
 def planes(matrices, block, potential):
@@ -402,11 +406,14 @@
     if whole_bands:
         share = potential.shape[0] // cuts
         mine = lax.dynamic_slice_in_dim(potential, lax.axis_index("cuts") * share, share, 0)
-        potential_all = lax.all_gather(mine.astype(BF16), ("cuts", "pencil"), axis=0, tiled=False)
-        potential_all = potential_all.reshape((cuts, pencils) + mine.shape)
+        shares = lax.all_gather(mine.astype(BF16), "pencil", axis=0, tiled=False)
     own = jnp.swapaxes(wavefunctions, 1, 2)
     neighbor = from_behind(own[bands_dev - EDGE :], "cuts", 1)
-    sums = lax.psum(edge_sums(neighbor, own), "pencil")
+    sums = edge_sums(neighbor, own)
+    if whole_bands:
+        shares, sums = lax.optimization_barrier((shares, sums))
+        potential_all = lax.all_gather(shares, "cuts", axis=0, tiled=False)
+    sums = lax.psum(sums, "pencil")
     weights = edge_weights(sums, keep_mask)
     places = (stick_map % rows_local) * box_size + stick_map // rows_local
     freq_rows = place(weights, places, own, neighbor)

time: 494 us -> 429 us (0.87)
  blocking collectives: 278 us -> 227 us
  Pallas kernels: 139 us -> 109 us
  waiting for transfers between devices: 27 us -> 41.3 us
    all_to_all x1, blocking collectives: 157 us -> 109 us  [hamiltonian_whole_bands(): lax.all_to_all(sent, 'pencil', split_axis=0, concat_axis=0, tiled=True)]
    pallas_call x1, Pallas kernels: 83 us -> 52.2 us  [planes(): pl.pallas_call(planes_kernel, grid=(count // per_step,), in_specs=[pl.Blo...]
    all_gather x1 -> x2, waiting for transfers between devices: 0.01 us -> 18.4 us  [the longest x1 18.4 us: local(): shares = lax.all_gather(mine.astype(BF16), 'pencil', axis=0, tiled=False)]
  transfers between devices with their start and end apart: 2 -> 3, of which waited for: 1 -> 2; matrix products, arithmetic and copies ran while one was open for 3% -> 4% of each run, Pallas kernels for 6% -> 7%
where the time goes in v2:
time: 429 us; the launch traced here: 427 us
  blocking collectives  227 us (53%)
  Pallas kernels  109 us (25%)
  waiting for transfers between devices  41.3 us (10%)
  local copies, waits for them, and re-layouts  32.1 us (7%)
  between operations  13.5 us (3%)
    all_to_all x1, blocking collectives, hamiltonian_whole_bands(): lax.all_to_all(result, 'pencil', split_axis=0, concat_axis=0, tiled=True)  109 us
    all_to_all x1, blocking collectives, hamiltonian_whole_bands(): lax.all_to_all(sent, 'pencil', split_axis=0, concat_axis=0, tiled=True)  109 us
    pallas_call x1, Pallas kernels, planes(): pl.pallas_call(planes_kernel, grid=(count // per_step,), in_specs=[pl.Blo...  52.2 us
    ppermute x1, waiting for transfers between devices, from_behind(): return lax.ppermute(block, axis, route)  22.8 us
    all_gather x1, waiting for transfers between devices, local(): shares = lax.all_gather(mine.astype(BF16), 'pencil', axis=0, tiled=False)  18.4 us
    pallas_call x1, Pallas kernels, place(): pl.pallas_call(place_kernel, grid=(steps,), in_specs=[pl.BlockSpec(memory...  17.6 us
    pallas_call x1, Pallas kernels, unplace(): pl.pallas_call(unplace_kernel, grid=(sticks_dev // width,), in_specs=[pl....  13.4 us
    pallas_call x1, local copies, waits for them, and re-layouts, first_ahead(): pl.pallas_call(first_ahead_kernel, grid=(columns // per_step,), in_specs=...  12.8 us
  transfers between devices with their start and end apart: 3, of which 2 were waited for; matrix products, arithmetic and copies ran while one was open for 4% of the time, Pallas kernels for 7%

profile of v2, /device:TPU:4, one launch (start us, length us, event | category | flops | bytes accessed | tf_op | source)
XLA Modules:
  0.0 426.6 jit_solution(442463973603557055)
XLA Ops:
  6.5 0.0 all-gather.5.cloned.1.call-start
  6.5 2.1 dynamic-slice_convert_fusion
  8.7 0.0 all-gather.5.cloned.1.call-update
  8.7 0.0 all-gather.7.cloned.1.call-start
  8.8 1.6 slice.40
  10.4 0.0 copy-start.1
  10.4 0.0 copy-start.2
  10.4 1.9 collective-permute-start
  12.3 22.8 %collective-permute-done.behind_ref = bf16[2,192,2304]{2,1,0:T(8,128)(2,1)S(1)} collective-permute-done((bf16[2,192,2304]{2,1,0:T(8,128)(2,1)S(1)}, bf16[2,192,2304]{2,1,0:T(8,128)(2,1)S(1)}, u32[]{:S(2)}, u32[]{:S(2)}) %collective-permute-start) | collective-permute-done | bytes 1769504 | tf_op jit(solution)/shard_map/ppermute | solution.py:20
  35.1 0.0 copy-start
  35.1 1.2 copy-done
  36.3 4.8 %shard_map.82 = f32[10,8,384]{2,1,0:T(8,128)} custom-call(bf16[2,192,2304]{2,1,0:T(8,128)(2,1)} %copy-done, bf16[4,192,2304]{2,1,0:T(8,128)(2,1)} %bitcast.42), custom_call_target="tpu_custom_call" | custom-call | tf_op jit(solution)/shard_map/pallas_call | solution.py:124
  41.2 1.1 reduce_sum.9
  42.2 18.4 %all-gather.5.cloned.1.call-done = bf16[24,192,192]{2,1,0:T(8,128)(2,1)} async-done(((bf16[6,192,192]{2,1,0:T(8,128)(2,1)}), bf16[24,192,192]{2,1,0:T(8,128)(2,1)}) %all-gather.5.cloned.1.call-update) | async-done | bytes 1769488 | tf_op jit(solution)/shard_map/all_gather | solution.py:409
  60.7 0.0 all-gather.7.cloned.1.call-update
  60.7 0.0 copy-done.1
  60.7 0.6 reshape.44.place_ref
  61.3 9.4 %psum.7 = f32[10]{0:T(128)S(1)} all-reduce(f32[10]{0:T(128)S(1)} %reduce_sum.9), channel_id=1, replica_groups=mesh['cuts'=8,'pencil'=4] {'pencil'}, use_global_device_ids=true, to_apply=%region_1.0 | all-reduce | flops 10 | bytes 80 | tf_op jit(solution)/shard_map/psum | solution.py:416
  70.8 0.1 fusion.7
  70.8 0.1 reshape.45
  70.9 0.1 copy.13
  71.0 0.1 reshape.46
  71.1 0.1 copy.14
  71.2 0.1 slice_add_fusion
  71.3 0.0 copy-done.2
  71.3 0.7 reshape.47.weight_ref
  71.9 17.6 %shard_map.83 = bf16[4,2304,192]{2,1,0:T(8,128)(2,1)} custom-call(f32[8]{0:T(128)} %reshape.47.weight_ref, s32[1,2304]{1,0:T(1,128)} %reshape.44.place_ref, bf16[4,192,2304]{2,1,0:T(8,128)(2,1)} %bitcast.43, bf16[2,192,2304]{2,1,0:T(8,128)(2,1)} %copy-done), custom_call_target="tpu_custom_call" | custom-call | tf_op jit(solution)/shard_map/pallas_call | solution.py:182
  89.6 108.8 %all_to_all.10 = bf16[4,24,96,192]{3,2,1,0:T(8,128)(2,1)} all-to-all(bf16[4,24,96,192]{3,2,1,0:T(8,128)(2,1)} %bitcast.46), channel_id=1, replica_groups=mesh['cuts'=8,'pencil'=4] {'pencil'}, dimensions={0} | all-to-all | bytes 7077888 | tf_op jit(solution)/shard_map/all_to_all | solution.py:365
  198.4 9.5 %shard_map.84 = bf16[96,192,192]{2,1,0:T(8,128)(2,1)} custom-call(bf16[192,192]{1,0:T(8,128)(2,1)} %constant.77.matrix_ref, bf16[96,96,192]{2,1,0:T(8,128)(2,1)} %bitcast.37), custom_call_target="tpu_custom_call" | custom-call | tf_op jit(solution)/shard_map/pallas_call | solution.py:242
  207.9 12.8 %copy.20 = bf16[96,192,192]{2,0,1:T(8,128)(2,1)} copy(bf16[96,192,192]{2,1,0:T(8,128)(2,1)} %shard_map.84) | data formatting | bytes 14155776 | tf_op jit(solution)/shard_map/pallas_call | solution.py:242
  220.7 0.0 all-gather.7.cloned.1.call-done
  220.7 52.2 %shard_map.85 = bf16[192,96,192]{2,1,0:T(8,128)(2,1)} custom-call(bf16[192,192]{1,0:T(8,128)(2,1)} %constant.62.last_re, bf16[192,192]{1,0:T(8,128)(2,1)} %constant.63.last_im, bf16[384,192]{1,0:T(8,128)(2,1)} %constant.69.mid_ahead, bf16[192,384]{1,0:T(8,128)(2,1)} %constant.73.mid_behind, bf16[192,192]{1,0:T(8,128)(2,1)} %constant.74.back_re, ...), custom_call_target="tpu_custom_call" | custom-call | tf_op jit(solution)/shard_map/pallas_call | solution.py:317
  272.9 12.7 %copy.19 = bf16[192,96,192]{2,0,1:T(8,128)(2,1)} copy(bf16[192,96,192]{2,1,0:T(8,128)(2,1)} %shard_map.85) | data formatting | bytes 14155776 | tf_op jit(solution)/shard_map/pallas_call | solution.py:317
  285.5 11.6 %shard_map.86 = bf16[96,96,192]{2,1,0:T(8,128)(2,1)} custom-call(bf16[96,384]{1,0:T(8,128)(2,1)} %constant.55.matrix_ref, bf16[96,192,192]{2,1,0:T(8,128)(2,1)} %bitcast.39, bf16[96,96,192]{2,1,0:T(8,128)(2,1)} %bitcast.38), custom_call_target="tpu_custom_call" | custom-call | tf_op jit(solution)/shard_map/pallas_call | solution.py:277
  297.1 109.2 %all_to_all.11 = bf16[4,24,96,192]{3,2,1,0:T(8,128)(2,1)} all-to-all(bf16[4,24,96,192]{3,2,1,0:T(8,128)(2,1)} %bitcast.47), channel_id=1, replica_groups=mesh['cuts'=8,'pencil'=4] {'pencil'}, dimensions={0} | all-to-all | bytes 7077888 | tf_op jit(solution)/shard_map/all_to_all | solution.py:371
  406.3 13.4 %shard_map.87 = bf16[4,192,2304]{2,1,0:T(8,128)(2,1)} custom-call(s32[1,2304]{1,0:T(1,128)} %reshape.44.place_ref, bf16[4,2304,192]{2,1,0:T(8,128)(2,1)} %bitcast.44), custom_call_target="tpu_custom_call" | custom-call | tf_op jit(solution)/shard_map/pallas_call | solution.py:217
  (3 shorter events, 0.0 us)
Async XLA Ops:
  6.5 54.1 %all-gather.5.cloned.1.call-start = ((), (), s32[]{:S(2)}) async-start(), calls=%async_computation.2 | async-start | bytes 2949120 | tf_op jit(solution)/shard_map/all_gather | solution.py:409
  8.7 212.0 %all-gather.7.cloned.1.call-start = ((), (), s32[]{:S(2)}) async-start(), calls=%async_computation.3 | async-start | bytes 21233664 | tf_op jit(solution)/shard_map/all_gather | solution.py:415
  10.4 50.3 %copy-start.1 = (s32[2304]{0:T(1024)S(1)}, s32[2304]{0:T(1024)}, u32[]{:S(2)}) copy-start(s32[2304]{0:T(1024)} %param.11) | copy-start | bytes 27652
  10.4 60.9 %copy-start.2 = (s32[1,2,2]{2,1,0:T(2,128)S(1)}, s32[1,2,2]{2,1,0:T(2,128)}, u32[]{:S(2)}) copy-start(s32[1,2,2]{2,1,0:T(2,128)} %param.10) | copy-start | bytes 52
  10.4 24.7 %collective-permute-start = (bf16[2,192,2304]{2,1,0:T(8,128)(2,1)S(1)}, bf16[2,192,2304]{2,1,0:T(8,128)(2,1)S(1)}, u32[]{:S(2)}, u32[]{:S(2)}) collective-permute-start(bf16[2,192,2304]{2,1,0:T(8,128)(2,1)S(1)} %slice.40), channel_id=1, source_target_pairs={{0,4},{4,8},{8,12},{12,16},{16,20},{20,24},{24,28},{1,5},{5,9},{9,... | collective-permute-start | bytes 5308424 | tf_op jit(solution)/shard_map/ppermute | solution.py:20
  35.1 1.2 copy-start
Sparse Core Ops, SparseCore 0:
  8.9 51.6 all-gather.4
  62.5 96.6 all-gather.6
